TPU v7x, 256 devices: a whole 4x4x8 slice. The times are simulated.
256 devices in a mesh: dp: 32 (over y_hi, z, core), proto: 8 (over y_lo, x).
Axes of the slice: x: 4, y: 4 (y_hi: 2, y_lo: 2; y = y_hi * 2 + y_lo), z: 8, core: 2. Of those that a mesh axis runs over, the one named last changes fastest.
Arguments:
- student_feats: bfloat16 [8192, 256], P('dp'), may hold values from -8 to 8
- teacher_feats: bfloat16 [2048, 256], P('dp'), may hold values from -8 to 8
- prototypes: bfloat16 [131072, 256], P('proto'), may hold values from -0.5 to 0.5
- pairs: int32 [8192, 2], P('dp'), may hold values from 0 to 63
- pair_mask: int32 [8192, 2], P('dp'), may hold values 0 or 1
- epoch: int32 [1], replicated, may hold values from 0 to 30
Outputs:
- loss_rows: float32 [8192], P('dp')
- grad_feats: float32 [8192, 256], P('dp')
- grad_proto: float32 [131072, 256], P(('proto', 'dp'))
Inputs may be any that keep to these rules, and one draw needn't show every extreme that they name: Entry p of row i names teacher crop (i // 256) * 64 + pairs[i, p].
All inputs are finite; a program needn't handle non-finite values. No bound on the sum of `pair_mask` on one device may be relied on, other than what follows from the above.
Results may differ from a plain program's by a relative error of at most 0.0027.
Values may be sent and summed in bfloat16 or wider, within the bound.
No kernel may reach another device: no remote copies, remote signals or barrier semaphores. Data moves between devices by JAX's collectives and lax.ppermute only.
A program may use at most 128 MiB of HBM per device.

v0:
```python
import jax
import jax.numpy as jnp
from jax import lax
from jax.experimental import pallas as pl
from jax.experimental.pallas import tpu as pltpu
from jax.sharding import Mesh, PartitionSpec as P

F32, BF16 = jnp.float32, jnp.bfloat16
YH, Z, C, YL, X = 2, 8, 2, 2, 4
NP = YL * X
D = 256
CR = 256
TE = 64
NT = YH * Z * C * TE
SH = 512
EPS = 1e-6
LOG2E = 1.4426950408889634
STUDENT = 10.0
SCALE = 2560.0
MIB = 1 << 20
KC, KR = 4, 256
CWS = 8


def dot(a, b, ca=1, cb=0, precision=None):
    return lax.dot_general(
        a, b, (((ca,), (cb,)), ((), ())), preferred_element_type=F32, precision=precision
    )


def unit(values):
    wide = values.astype(F32)
    inv = lax.rsqrt(jnp.sum(wide * wide, axis=1, keepdims=True) + EPS)
    return wide * inv, inv


def params(mib):
    return pltpu.CompilerParams(vmem_limit_bytes=mib * MIB, dimension_semantics=("arbitrary",))


def hbm(x):
    return pltpu.with_memory_space_constraint(x, pltpu.HBM)


ANY = pl.BlockSpec(memory_space=pl.ANY)


def call(body, idx, grid, ins, in_specs, outs, out_specs, scratch=(), mib=24, flops=0, nbytes=0, alias={}):
    return pl.pallas_call(
        body,
        grid_spec=pltpu.PrefetchScalarGridSpec(
            num_scalar_prefetch=1,
            grid=(grid,),
            in_specs=in_specs,
            out_specs=out_specs,
            scratch_shapes=list(scratch),
        ),
        out_shape=outs,
        compiler_params=params(mib),
        input_output_aliases=alias,
        cost_estimate=pl.CostEstimate(flops=flops, bytes_accessed=nbytes, transcendentals=0),
    )(idx, *ins)


def loop(n, body):
    lax.fori_loop(0, n, lambda k, x: (body(k), x)[1], 0)


def copier(source, target, sem):
    return lambda k: pltpu.make_async_copy(source(k), target(k), sem.at[k])


def start_all(n, copy):
    loop(n, lambda k: copy(k).start())


def wait_all(n, copy):
    loop(n, lambda k: copy(k).wait())


def sems(n):
    return pltpu.SemaphoreType.DMA((n,))


def whole(shape):
    zeros = (0,) * len(shape)
    return pl.BlockSpec(shape, lambda i, s: zeros)


def spec(shape, fn):
    return pl.BlockSpec(shape, fn)


def sds(shape, dtype):
    return jax.ShapeDtypeStruct(shape, dtype)


def selector(pairs, mask):
    rows = lax.broadcasted_iota(jnp.int32, (TE, CR), 0)
    m = mask[...].astype(F32)
    return jnp.where(pairs[0:1, :] == rows, m[0:1, :], 0.0) + jnp.where(
        pairs[1:2, :] == rows, m[1:2, :], 0.0
    )


def prep_body(s, sf, tf, pairs, mask, spay, trep):
    zs, _ = unit(sf[...])
    zsb = zs.astype(BF16)
    spay[0:CR, :] = zsb
    spay[CR : CR + TE, :] = dot(selector(pairs, mask).astype(BF16), zsb).astype(BF16)
    zt, _ = unit(tf[...])
    ztb = zt.astype(BF16)
    for b in range(YH * Z):
        trep[b] = ztb


def norm_body(s, w, after, out, done, wv, nv, si, so):
    n = YH * Z
    ins = copier(lambda j: w.at[j, s[2]], lambda j: wv.at[j], si)
    outs = copier(lambda j: nv.at[j], lambda j: out.at[j], so)
    start_all(n, ins)

    def step(j):
        ins(j).wait()
        wn, _ = unit(wv[j])
        nv[j] = wn.astype(BF16)
        outs(j).start()

    loop(n, step)
    done[...] = jnp.zeros_like(done)
    wait_all(n, outs)


def e_step(wb, z_refs, g, tacc):
    for q in range(2):
        rows = slice(q * CR, (q + 1) * CR)
        e = jnp.exp2(dot(z_refs[q][0:CR, :], wb, 1, 1) * (STUDENT * LOG2E))
        t = e[:, 0:128]
        for k in range(1, SH // 128):
            t = t + e[:, k * 128 : (k + 1) * 128]
        tacc[rows, :] += t
        g[rows, :] += dot(e.astype(BF16), wb)


def put_totals(s, yy, tacc, trow):
    yh, c = s[0], s[2]
    for q in range(2):
        t = jnp.sum(tacc[q * CR : (q + 1) * CR, :].T, axis=0, keepdims=True)
        trow[pl.ds((yh ^ yy) * 2 + (c ^ q), 1), :] = t


def e1_body(s, w, b00, b01, mask, keep, trow, wnb, tacc):
    @pl.when(pl.program_id(0) == 0)
    def _():
        keep[...] = jnp.zeros_like(keep)
        tacc[...] = jnp.zeros_like(tacc)

    for j in range(2):
        wn, _ = unit(w[j, 0])
        wb = wn.astype(BF16)
        wnb[j] = wb
        e_step(wb, (b00, b01), keep, tacc)

    @pl.when(pl.program_id(0) == pl.num_programs(0) - 1)
    def _():
        trow[...] = jnp.zeros_like(trow)
        put_totals(s, 0, tacc, trow)
        m = mask[...].astype(F32)
        trow[pl.ds(s[0] * 2 + s[2] + 8, 1), :] = (m[0:1, :] + m[1:2, :]) * (1.0 / NP)


def e2_body(s, w, b10, b11, trow1, send, trow, tacc, wv, si):
    ins = copier(lambda j: w.at[j], lambda j: wv.at[j], si)
    start_all(Z, ins)
    send[...] = jnp.zeros_like(send)
    tacc[...] = jnp.zeros_like(tacc)
    for j in range(Z):
        ins(j).wait()
        e_step(wv[j], (b10, b11), send, tacc)
    trow[...] = trow1[...]
    put_totals(s, 1, tacc, trow)
    send[2 * CR : 2 * CR + 16, :] = trow[...]


def put_rows(racc, rsc):
    for k in range(8):
        rsc[k : k + 1, :] = racc[0:1, k * 256 : (k + 1) * 256]


def k_body(s, w, za, zb, epoch, after, b00, b10, kt, rz, group, racc, rsc, so):
    i = pl.program_id(0)

    size = CR + TE
    outs = [
        pltpu.make_async_copy(blk, group.at[pl.ds(q * size, size), :], so.at[q])
        for q, blk in enumerate((b00, b10))
    ]

    @pl.when(i == 0)
    def _():
        for copy in outs:
            copy.start()
        racc[...] = jnp.zeros_like(racc)

    tau = 0.04 + 0.001 * epoch[0:1, 0:1].astype(F32)
    factor = LOG2E / tau
    wn, _ = unit(w[...])
    wb = wn.astype(BF16)
    half = NT // 2
    ka = jnp.exp2(dot(wb, za[...], 1, 1) * factor)
    kb = jnp.exp2(dot(wb, zb[...], 1, 1) * factor)
    kt[0, :, 0:half] = ka
    kt[0, :, half:NT] = kb
    c = 1.0 / (jnp.sum(ka, axis=1, keepdims=True) + jnp.sum(kb, axis=1, keepdims=True))
    racc[0:1, 0:half] += jnp.sum(ka * c, axis=0, keepdims=True)
    racc[0:1, half:NT] += jnp.sum(kb * c, axis=0, keepdims=True)

    @pl.when(i == pl.num_programs(0) - 1)
    def _():
        put_rows(racc, rsc)
        for b in range(Z):
            rz[b] = rsc[...]
        for copy in outs:
            copy.wait()


def mid1_body(s, rz, tpk, tin, after, out):
    r = jnp.sum(rz[...], axis=0)
    ab = tpk[...] + tin[2 * CR : 2 * CR + 16, :]
    for b in range(C * NP):
        out[b, 0:8, :] = r
        out[b, 8:12, :] = ab[0:4]
        out[b, 12:16, :] = ab[8:12]


def mid2_body(s, rz, keep, tin, out, g):
    c = s[2]
    r = jnp.sum(rz[:, 0:8, :], axis=0)
    g[...] = keep[...] + tin[0 : 2 * CR, :]
    for cd in range(C):
        for p in range(NP):
            out[cd * NP + p, 0:8, :] = r
            out[cd * NP + p, 8:40, :] = g[pl.ds((c ^ cd) * CR + p * 32, 32), :]


def row_total(s, got, sc):
    c = s[2]
    same = jnp.zeros((8, D), F32)
    other = jnp.zeros((8, D), F32)
    for p in range(NP):
        same = same + got[c * NP + p, 0:8, :]
        other = other + got[(1 - c) * NP + p, 0:8, :]
    sc[0:4, :] = same[0:4] + other[4:8]
    sc[4:8, :] = same[4:8] + other[0:4]


def scales(s, got, rsc, u):
    row_total(s, got, rsc)
    inv = 1.0 / rsc[...]
    for k in range(8):
        u[0:1, k * 256 : (k + 1) * 256] = inv[k : k + 1, :]


def it2_body(s, kt, got, rz, racc, rsc, u, a, kv, si):
    ins = copier(lambda k: kt.at[k], lambda k: kv.at[k], si)
    start_all(KC, ins)
    racc[...] = jnp.zeros_like(racc)
    scales(s, got, rsc, u)
    tot = jnp.sum(got[:, 8:16, :], axis=0)
    a[0:4, :] = tot[4:8] / tot[0:4]
    a[4:8, :] = tot[4:8]

    def step(j):
        ins(j).wait()
        k = kv[j]
        c = 1.0 / jnp.sum(k * u[...], axis=1, keepdims=True)
        racc[...] += jnp.sum(k * c, axis=0, keepdims=True)

    loop(KC, step)
    put_rows(racc, rsc)
    for b in range(Z):
        rz[b, 0:8, :] = rsc[...]
        rz[b, 8:16, :] = a[...]


def it3_body(s, kt, got, rz, ccol, racc, rsc, u, crow, kv, si):
    ins = copier(lambda k: kt.at[k], lambda k: kv.at[k], si)
    start_all(KC, ins)
    racc[...] = jnp.zeros_like(racc)
    crow[...] = jnp.zeros_like(crow)
    scales(s, got, rsc, u)

    def step(j):
        ins(j).wait()
        k = kv[j]
        ku = k * u[...]
        t = ku[:, 0:128]
        for a in range(1, NT // 128):
            t = t + ku[:, a * 128 : (a + 1) * 128]
        c = 1.0 / jnp.sum(t, axis=1, keepdims=True)
        ccol[j] = jnp.broadcast_to(c, (KR, 128))
        crow[pl.ds(j, 1), :] = 1.0 / jnp.sum(t.T, axis=0, keepdims=True)
        racc[...] += jnp.sum(k * c, axis=0, keepdims=True)

    loop(KC, step)
    put_rows(racc, rsc)
    for b in range(Z):
        rz[b, 0:8, :] = rsc[...]
        rz[b, 8:16, :] = crow[...]


def gw_body(s, w, h_own, h_other, rz, after, out, done, wb):
    yh, c = s[0], s[2]

    @pl.when(pl.program_id(0) == 0)
    def _():
        wn, _ = unit(w[...])
        wb[...] = wn.astype(BF16)
        out[...] = jnp.zeros_like(out)
        done[...] = jnp.zeros_like(done)

    for j in range(2):
        acc = None
        for q in range(4):
            zq = (h_own, h_other)[q % 2][j, (q // 2) * (CR + TE) : (q // 2) * (CR + TE) + CR, :]
            at = 8 + (yh ^ (q // 2)) * 2 + (c ^ (q % 2))
            a = rz[pl.program_id(0) * 2 + j, pl.ds(at, 1), :]
            e = jnp.exp2(dot(wb[...], zq, 1, 1) * (STUDENT * LOG2E)) * a
            part = dot(e.astype(BF16), zq)
            acc = part if acc is None else acc + part
        out[...] += acc


def cw_body(s, w, za, zb, epoch, rz, after, keep, send, zp, acc):
    i = pl.program_id(0)
    c = s[2]

    @pl.when(i == 0)
    def _():
        zp[0:TE, :] = za[...]
        zp[TE : 2 * TE, :] = zb[...]
        acc[...] = jnp.zeros_like(acc)

    factor = LOG2E / (0.04 + 0.001 * epoch[0:1, 0:1].astype(F32))
    part = None
    for j in range(CWS):
        wb = w[j]
        e = jnp.exp2(dot(zp[...], wb, 1, 1) * factor)
        at = i * CWS + j
        yy, zz = at // Z, at % Z
        for h in range(2):
            row = rz[zz, pl.ds(8 + 2 * yy + h, 1), :]
            codes = (e[:, h * 256 : (h + 1) * 256] * row).astype(BF16)
            one = dot(codes, wb[h * 256 : (h + 1) * 256])
            part = one if part is None else part + one
    acc[...] += part

    @pl.when(i == pl.num_programs(0) - 1)
    def _():
        r = jnp.sum(rz[:, 0:8, :], axis=0)
        keep[0:8, :] = r
        keep[8 : 8 + TE, :] = acc[0:TE, :]
        send[0:4, :] = r[4:8]
        send[4:8, :] = r[0:4]
        send[8 : 8 + TE, :] = acc[TE : 2 * TE, :]


def mid3_body(s, keep, tin, got2, out):
    pack = keep[...] + tin[...]
    g = jnp.sum(got2[:, 8:40, :], axis=0)
    for p in range(NP):
        out[p, 0:72, :] = pack
        out[p, 72:104, :] = g


def last_body(
    s, sf, pairs, mask, got1, got3, kt, ccol, h_own, h_other, gwp, w,
    loss, feats, protos,
    rsc, trow, g, hv, kv, cv, u_all, si,
):
    n = KC // YH
    ks = copier(lambda k: kt.at[s[0] * n + k], lambda k: kv.at[k], si)
    start_all(n, ks)

    def crops(h, cc):
        def copy(at):
            block = (at // Z) ^ s[0]
            to = cc * YH * Z + at
            return pltpu.make_async_copy(
                h.at[at % Z, pl.ds(block * (CR + TE) + CR, TE), :],
                hv.at[pl.ds(to * TE, TE), :],
                si.at[n + to],
            )

        return copy

    crops_own, crops_other = crops(h_own, 0), crops(h_other, 1)
    start_all(YH * Z, crops_own)
    start_all(YH * Z, crops_other)
    more = pltpu.make_async_copy(ccol.at[pl.ds(s[0] * n, n)], cv, si.at[n + 32])
    more.start()

    yh, z, c = s[0], s[1], s[2]
    zs, inv = unit(sf[...])
    zsb = zs.astype(BF16).astype(F32)
    trow[...] = jnp.sum(got1[:, 8:16, :], axis=0)
    at = yh * 2 + c
    t = trow[pl.ds(at, 1), :]
    msum = trow[pl.ds(at + 4, 1), :]
    a = jnp.broadcast_to(msum / t, (128, CR)).T[:, 0:1]
    rsc[...] = 1.0 / jnp.sum(got3[:, 0:8, :], axis=0)
    own = yh * Z + z
    row = rsc[pl.ds(own // 4, 1), :]
    u = row[:, 0:128]
    u = jnp.where(own % 4 >= 2, row[:, 128:256], u)
    col = jnp.broadcast_to(u, (128, 128)).T
    ucol = jnp.where(own % 2 == 1, col[TE : 2 * TE, 0:1], col[0:TE, 0:1])
    cw = jnp.sum(got3[:, 8:72, :], axis=0) * ucol
    for p in range(NP):
        g[p * 32 : (p + 1) * 32, :] = got3[p, 72:104, :]
    q = dot(selector(pairs, mask), cw, 0, 0, lax.Precision.HIGHEST)
    cross = dot(jnp.ones((8, D), F32), zsb * q, 1, 1, lax.Precision.HIGHEST)
    loss[...] = msum * jnp.log(t) - STUDENT * cross[0:1, :]
    gz = SCALE * (a * g[...] - q)
    feats[...] = (gz - zs * jnp.sum(zs * gz, axis=1, keepdims=True)) * inv

    for k in range(8):
        u_all[0:1, k * D : (k + 1) * D] = rsc[k : k + 1, :]
    wait_all(YH * Z, crops_own)
    wait_all(YH * Z, crops_other)
    more.wait()

    def step(k):
        ks(k).wait()
        acc = dot((kv[k] * u_all[...]).astype(BF16), hv[...])
        rows = pl.ds(k * KR, KR)
        wn, inv_w = unit(w[rows, :])
        gw = SCALE * (gwp[rows, :] - acc * cv[k, :, 0:1])
        protos[rows, :] = (gw - wn * jnp.sum(wn * gw, axis=1, keepdims=True)) * inv_w

    loop(n, step)


def local(student, teacher, prototypes, pairs, mask, epoch):
    yh, z, c = lax.axis_index("yh"), lax.axis_index("z"), lax.axis_index("c")
    p = lax.axis_index(("yl", "x"))
    idx = jnp.stack([yh, z, c, p]).astype(jnp.int32)
    ep = epoch.reshape(1, 1)
    student, teacher, protos = hbm(student), hbm(teacher), hbm(prototypes)
    pairs, mask = hbm(pairs.T), hbm(mask.T)
    chunked = hbm(prototypes.reshape(YH * Z, C, SH, D))
    swap = [(0, 1), (1, 0)]
    prc = ("c", "yl", "x")

    spay, trep = call(
        prep_body, idx, 1,
        (student, teacher, pairs, mask),
        [whole((CR, D)), whole((TE, D)), whole((2, CR)), whole((2, CR))],
        [sds((CR + TE, D), BF16), sds((YH * Z, TE, D), BF16)],
        [whole((CR + TE, D)), whole((YH * Z, TE, D))],
        nbytes=1 << 20,
    )
    b00 = spay
    b01 = lax.ppermute(b00, "c", swap)
    b10 = lax.ppermute(b00, "yh", swap)
    za = lax.all_to_all(trep, ("yh", "z"), 0, 0, tiled=True).reshape(NT // 2, D)
    wbuf = pltpu.VMEM((Z, SH, D), BF16)
    tbuf = pltpu.VMEM((2 * CR, 128), F32)
    half = Z // 2
    pair_spec = spec((2, SH, D), lambda i, s: (i, 0, 0))
    keep, trow1, wnb = call(
        e1_body, idx, half,
        (chunked, b00, b01, mask),
        [spec((2, 1, SH, D), lambda i, s: (s[0] * half + i, s[2], 0, 0))]
        + [whole((CR + TE, D))] * 2
        + [whole((2, CR))],
        [sds((2 * CR, D), F32), sds((16, D), F32), pltpu.HBM((Z, SH, D), BF16)],
        [whole((2 * CR, D)), whole((16, D)), pair_spec],
        [tbuf], flops=4 << 30, nbytes=4 << 20,
    )
    b10, trow1 = lax.optimization_barrier((b10, trow1))
    b11 = lax.ppermute(b10, "c", swap)
    send, tpk = call(
        e2_body, idx, 1,
        (hbm(wnb), b10, b11, trow1),
        [ANY] + [whole((CR + TE, D))] * 2 + [whole((16, D))],
        [sds((2 * CR + 16, D), F32), sds((16, D), F32)],
        [whole((2 * CR + 16, D)), whole((16, D))],
        [tbuf, wbuf, sems(Z)], flops=4 << 30, nbytes=4 << 20,
    )
    tin = lax.ppermute(send, "yh", swap)
    za, tpk = lax.optimization_barrier((za, tpk))
    zb = lax.ppermute(za, "c", swap)

    kbuf = pltpu.VMEM((KC, KR, NT), F32)
    kt_spec = spec((1, KR, NT), lambda i, s: (i, 0, 0))
    per = SH // KR
    kt, rz1, group = call(
        k_body, idx, KC,
        (protos, za, zb, ep, tpk, b00, b10),
        [
            spec((KR, D), lambda i, s: ((((i // per) * Z + s[1]) * C + s[2]) * per + i % per, 0)),
            whole((NT // 2, D)), whole((NT // 2, D)), whole((1, 1)), ANY, ANY, ANY,
        ],
        [
            pltpu.HBM((KC, KR, NT), F32), sds((Z, 8, D), F32),
            pltpu.HBM((2 * (CR + TE), D), BF16),
        ],
        [kt_spec, whole((Z, 8, D)), ANY],
        [pltpu.VMEM((1, NT), F32), pltpu.VMEM((8, D), F32), sems(2)],
        flops=4 << 30, nbytes=10 << 20,
    )
    h_own = lax.all_gather(group, "z", axis=0, tiled=False)
    wall = pltpu.VMEM((YH * Z, SH, D), BF16)
    wnc, done = call(
        norm_body, idx, 1,
        (chunked, rz1),
        [ANY, ANY],
        [pltpu.HBM((YH * Z, SH, D), BF16), sds((8, 128), F32)],
        [ANY, whole((8, 128))],
        [wall, wall, sems(YH * Z), sems(YH * Z)],
        flops=2 << 30, nbytes=8 << 20,
    )
    rz1 = lax.all_to_all(rz1, "z", 0, 0, tiled=True)
    pay1 = call(
        mid1_body, idx, 1,
        (rz1, tpk, tin, done),
        [whole((Z, 8, D)), whole((16, D)), whole((2 * CR + 16, D)), ANY],
        sds((C * NP, 16, D), F32), whole((C * NP, 16, D)),
        nbytes=1 << 19,
    )
    got1 = lax.all_to_all(pay1, prc, 0, 0, tiled=True)

    it_scratch = [pltpu.VMEM((1, NT), F32), pltpu.VMEM((8, D), F32), pltpu.VMEM((1, NT), F32)]
    rz2 = call(
        it2_body, idx, 1,
        (hbm(kt), got1),
        [ANY, whole((C * NP, 16, D))],
        sds((Z, 16, D), F32), whole((Z, 16, D)),
        it_scratch + [pltpu.VMEM((8, D), F32), kbuf, sems(KC)], nbytes=9 << 20,
    )
    rz2 = lax.all_to_all(rz2, "z", 0, 0, tiled=True)
    pay2 = call(
        mid2_body, idx, 1,
        (rz2, keep, tin),
        [whole((Z, 16, D)), whole((2 * CR, D)), whole((2 * CR + 16, D))],
        sds((C * NP, 40, D), F32), whole((C * NP, 40, D)),
        [pltpu.VMEM((2 * CR, D), F32)],
        nbytes=2 << 20,
    )
    got2 = lax.all_to_all(pay2, prc, 0, 0, tiled=True)
    h_own, got2 = lax.optimization_barrier((h_own, got2))
    h_other = lax.ppermute(h_own, "c", swap)
    rz3, ccol = call(
        it3_body, idx, 1,
        (hbm(kt), got2),
        [ANY, whole((C * NP, 40, D))],
        [sds((Z, 16, D), F32), pltpu.HBM((KC, KR, 128), F32)],
        [whole((Z, 16, D)), whole((KC, KR, 128))],
        it_scratch + [pltpu.VMEM((8, D), F32), kbuf, sems(KC)], nbytes=9 << 20,
    )
    gwp, done3 = call(
        gw_body, idx, half,
        (protos, hbm(h_own), hbm(h_other), rz2, rz3),
        [
            spec((SH, D), lambda i, s: ((s[0] * Z + s[1]) * C + s[2], 0)),
            spec((2, 2 * (CR + TE), D), lambda i, s: (i, 0, 0)),
            spec((2, 2 * (CR + TE), D), lambda i, s: (i, 0, 0)),
            whole((Z, 16, D)), ANY,
        ],
        [sds((SH, D), F32), sds((8, 128), F32)],
        [whole((SH, D)), whole((8, 128))],
        [pltpu.VMEM((SH, D), BF16)],
        flops=8 << 30, nbytes=8 << 20,
    )
    rz3 = lax.all_to_all(rz3, "z", 0, 0, tiled=True)
    keep3, send3 = call(
        cw_body, idx, YH * Z // CWS,
        (hbm(wnc), za, zb, ep, rz3, done3),
        [
            spec((CWS, SH, D), lambda i, s: (i, 0, 0)),
            spec((TE, D), lambda i, s: (s[0] * Z + s[1], 0)),
            spec((TE, D), lambda i, s: (s[0] * Z + s[1], 0)),
            whole((1, 1)), whole((Z, 16, D)), ANY,
        ],
        [sds((8 + TE, D), F32)] * 2, [whole((8 + TE, D))] * 2,
        [pltpu.VMEM((2 * TE, D), BF16), pltpu.VMEM((2 * TE, D), F32)],
        flops=1 << 30, nbytes=6 << 20,
    )
    tin3 = lax.ppermute(send3, "c", swap)
    pay3 = call(
        mid3_body, idx, 1,
        (keep3, tin3, got2),
        [whole((8 + TE, D))] * 2 + [whole((C * NP, 40, D))],
        sds((NP, 104, D), F32), whole((NP, 104, D)),
        nbytes=2 << 20,
    )
    got3 = lax.all_to_all(pay3, ("yl", "x"), 0, 0, tiled=True)

    n = KC // YH
    loss, grad_feats, grad_proto = call(
        last_body, idx, 1,
        (student, pairs, mask, got1, got3, hbm(kt), hbm(ccol), hbm(h_own), hbm(h_other), gwp, protos),
        [
            whole((CR, D)), whole((2, CR)), whole((2, CR)),
            whole((C * NP, 16, D)), whole((NP, 104, D)),
            ANY, ANY, ANY, ANY, whole((SH, D)),
            spec((SH, D), lambda i, s: ((s[0] * Z + s[1]) * C + s[2], 0)),
        ],
        [sds((1, CR), F32), sds((CR, D), F32), sds((SH, D), F32)],
        [whole((1, CR)), whole((CR, D)), whole((SH, D))],
        [
            pltpu.VMEM((8, D), F32), pltpu.VMEM((8, D), F32), pltpu.VMEM((CR, D), F32),
            pltpu.VMEM((NT, D), BF16), pltpu.VMEM((n, KR, NT), F32),
            pltpu.VMEM((n, KR, 128), F32), pltpu.VMEM((1, NT), F32), sems(n + 33),
        ],
        flops=1 << 30, nbytes=8 << 20,
    )
    return loss.reshape(CR), grad_feats, grad_proto


def solution(mesh):
    fine = Mesh(mesh.devices.reshape(YH, Z, C, YL, X), ("yh", "z", "c", "yl", "x"))
    dp, proto = ("yh", "z", "c"), ("yl", "x")
    in_specs = (P(dp, None), P(dp, None), P(proto, None), P(dp, None), P(dp, None), P())
    out_specs = (P(dp), P(dp, None), P(proto + dp, None))
    return jax.shard_map(local, mesh=fine, in_specs=in_specs, out_specs=out_specs, check_vma=False)
```

profile of v0, /device:TPU:1, one launch (start us, length us, event | category | flops | bytes accessed | tf_op | source)
XLA Modules:
  0.0 170.1 jit_solution(12999444502903756738)
XLA Ops:
  7.2 0.1 pad_add_fusion.s
  7.3 2.5 %shard_map.85 = (bf16[320,256]{1,0:T(8,128)(2,1)S(1)}, bf16[16,64,256]{2,1,0:T(8,128)(2,1)}) custom-call(s32[4]{0:T(128)S(1)} %pad_add_fusion.s, bf16[256,256]{1,0:T(8,128)(2,1)} %sf.3, bf16[64,256]{1,0:T(8,128)(2,1)} %tf.1, s32[2,256]{1,0:T(2,128)} %bitcast.21, s32[2,256]{1,0:T(2,128)} %bitcast.23), custom_call_target="tpu_custom_call" | custom-call | bytes 1048576 | tf_op jit(solution)/shard_map/pallas_call | solution.py:49
  9.7 3.2 %collective-permute-start = (bf16[320,256]{1,0:T(8,128)(2,1)S(1)}, bf16[320,256]{1,0:T(8,128)(2,1)S(1)}, u32[]{:S(2)}, u32[]{:S(2)}) collective-permute-start(bf16[320,256]{1,0:T(8,128)(2,1)S(1)} %get-tuple-element.31.b00), channel_id=1, source_target_pairs={{0,8},{8,0},{1,9},{9,1},{2,10},{10,2},{3,11},{11,3},{4,12},{12,4},... | collective-permute-start | bytes 491528 | tf_op jit(solution)/shard_map/ppermute | solution.py:464
  12.9 9.2 %all-to-all-start = ((bf16[16,64,256]{2,1,0:T(8,128)(2,1)}), bf16[16,64,256]{2,1,0:T(8,128)(2,1)S(1)}, u32[]{:S(2)}, u32[]{:S(2)}) async-start(bf16[16,64,256]{2,1,0:T(8,128)(2,1)} %get-tuple-element.30), calls=%async_computation | async-start | bytes 1048576 | tf_op jit(solution)/shard_map/all_to_all | solution.py:466
  22.2 3.0 %collective-permute-start.1 = (bf16[320,256]{1,0:T(8,128)(2,1)S(1)}, bf16[320,256]{1,0:T(8,128)(2,1)S(1)}, u32[]{:S(2)}, u32[]{:S(2)}) collective-permute-start(bf16[320,256]{1,0:T(8,128)(2,1)S(1)} %get-tuple-element.31.b00), channel_id=1, source_target_pairs={{0,128},{128,0},{1,129},{129,1},{2,130},{130,2},{3,131},{131,3},{4... | collective-permute-start | bytes 491528 | tf_op jit(solution)/shard_map/ppermute | solution.py:465
  25.1 6.8 %shard_map.86 = (f32[512,256]{1,0:T(8,128)S(1)}, f32[16,256]{1,0:T(8,128)S(1)}, bf16[8,512,256]{2,1,0:T(8,128)(2,1)}) custom-call(s32[4]{0:T(128)S(1)} %pad_add_fusion.s, bf16[16,2,512,256]{3,2,1,0:T(8,128)(2,1)} %bitcast.16, bf16[320,256]{1,0:T(8,128)(2,1)S(1)} %get-tuple-element.31.b00, bf16[320,256]{1,0:T(8,128)(2,1)S(1)} %collective-permute-done.b01, ...), custom_call_target="tpu_custom_call" | custom-call | flops 4294967296 | bytes 4194304 | tf_op jit(solution)/shard_map/pallas_call | solution.py:49
  31.9 1.2 collective-permute-start.2
  33.1 1.0 collective-permute-done.2.b11
  34.1 5.4 %shard_map.87 = (f32[528,256]{1,0:T(8,128)S(1)}, f32[16,256]{1,0:T(8,128)S(1)}) custom-call(s32[4]{0:T(128)S(1)} %pad_add_fusion.s, bf16[8,512,256]{2,1,0:T(8,128)(2,1)} %get-tuple-element.32.w, bf16[320,256]{1,0:T(8,128)(2,1)S(1)} %collective-permute-done.1.b10, bf16[320,256]{1,0:T(8,128)(2,1)S(1)} %collective-permute-done.2.b11, ...), custom_call_target="tpu_custom_call" | custom-call | flops 4294967296 | bytes 4194304 | tf_op jit(solution)/shard_map/pallas_call | solution.py:49
  39.6 0.5 collective-permute-start.3
  40.7 0.9 collective-permute-done.3.zb
  41.6 6.7 %shard_map.88 = (f32[4,256,2048]{2,1,0:T(8,128)}, f32[8,8,256]{2,1,0:T(8,128)}, bf16[640,256]{1,0:T(8,128)(2,1)}) custom-call(s32[4]{0:T(128)S(1)} %pad_add_fusion.s, bf16[16384,256]{1,0:T(8,128)(2,1)} %w.5, bf16[1024,256]{1,0:T(8,128)(2,1)S(1)} %bitcast.14, bf16[1024,256]{1,0:T(8,128)(2,1)S(1)} %collective-permute-done.3.zb, s32[1,1]{1,0:T(1,128)} %bitcast.11.epoch, ...), custom_call_target="tpu_custom_call" | custom-call | flops 4294967296 | bytes 10485760 | tf_op jit(solution)/shard_map/pallas_call | solution.py:49
  48.2 3.0 %collective-permute-start.4 = (f32[528,256]{1,0:T(8,128)S(1)}, f32[528,256]{1,0:T(8,128)S(1)}, u32[]{:S(2)}, u32[]{:S(2)}) collective-permute-start(f32[528,256]{1,0:T(8,128)S(1)} %get-tuple-element.40), channel_id=1, source_target_pairs={{0,128},{128,0},{1,129},{129,1},{2,130},{130,2},{3,131},{131,3},{4... | collective-permute-start | bytes 1622024 | tf_op jit(solution)/shard_map/ppermute | solution.py:491
  51.2 7.3 %all-to-all-start.1 = ((f32[8,8,256]{2,1,0:T(8,128)}), f32[8,8,256]{2,1,0:T(8,128)S(1)}, u32[]{:S(2)}, u32[]{:S(2)}) async-start(f32[8,8,256]{2,1,0:T(8,128)} %get-tuple-element.39.after), calls=%async_computation.1 | async-start | bytes 131072 | tf_op jit(solution)/shard_map/all_to_all | solution.py:524
  58.6 5.0 %shard_map.89 = (bf16[16,512,256]{2,1,0:T(8,128)(2,1)}, f32[8,128]{1,0:T(8,128)S(1)}) custom-call(s32[4]{0:T(128)S(1)} %pad_add_fusion.s, bf16[16,2,512,256]{3,2,1,0:T(8,128)(2,1)} %bitcast.17, f32[8,8,256]{2,1,0:T(8,128)} %get-tuple-element.39.after), custom_call_target="tpu_custom_call" | custom-call | flops 2147483648 | bytes 8388608 | tf_op jit(solution)/shard_map/pallas_call | solution.py:49
  63.6 2.3 %all-to-all-done.1.rz = f32[8,8,256]{2,1,0:T(8,128)S(1)} async-done(((f32[8,8,256]{2,1,0:T(8,128)}), f32[8,8,256]{2,1,0:T(8,128)S(1)}, u32[]{:S(2)}, u32[]{:S(2)}) %all-to-all-start.1) | async-done | bytes 65568 | tf_op jit(solution)/shard_map/all_to_all | solution.py:524
  65.9 0.6 shard_map.90
  66.5 14.1 %all_to_all.35.got.got1 = f32[16,16,256]{2,1,0:T(8,128)S(1)} all-to-all(f32[16,16,256]{2,1,0:T(8,128)S(1)} %shard_map.90), channel_id=1, replica_groups=mesh['yh'=2,'z'=8,'c'=2,'yl'=2,'x'=4] {'c','yl','x'}, dimensions={0} | all-to-all | bytes 524288 | tf_op jit(solution)/shard_map/all_to_all | solution.py:532
  80.5 4.5 %shard_map.91 = f32[8,16,256]{2,1,0:T(8,128)S(1)} custom-call(s32[4]{0:T(128)S(1)} %pad_add_fusion.s, f32[4,256,2048]{2,1,0:T(8,128)} %get-tuple-element.43.kt, f32[16,16,256]{2,1,0:T(8,128)S(1)} %all_to_all.35.got.got1), custom_call_target="tpu_custom_call" | custom-call | bytes 9437184 | tf_op jit(solution)/shard_map/pallas_call | solution.py:49
  85.0 13.0 %all_to_all.36.rz = f32[8,16,256]{2,1,0:T(8,128)S(1)} all-to-all(f32[8,16,256]{2,1,0:T(8,128)S(1)} %shard_map.91), channel_id=1, replica_groups=mesh['yh'=2,'z'=8,'c'=2,'yl'=2,'x'=4] {'z'}, dimensions={0} | all-to-all | bytes 262144 | tf_op jit(solution)/shard_map/all_to_all | solution.py:542
  98.0 0.6 shard_map.92
  98.7 16.3 %all_to_all.37.got.got2 = f32[16,40,256]{2,1,0:T(8,128)S(1)} all-to-all(f32[16,40,256]{2,1,0:T(8,128)S(1)} %shard_map.92), channel_id=1, replica_groups=mesh['yh'=2,'z'=8,'c'=2,'yl'=2,'x'=4] {'c','yl','x'}, dimensions={0} | all-to-all | bytes 1310720 | tf_op jit(solution)/shard_map/all_to_all | solution.py:551
  115.0 0.2 collective-permute-start.5
  115.2 5.2 %shard_map.93 = (f32[8,16,256]{2,1,0:T(8,128)}, f32[4,256,128]{2,1,0:T(8,128)}) custom-call(s32[4]{0:T(128)S(1)} %pad_add_fusion.s, f32[4,256,2048]{2,1,0:T(8,128)} %get-tuple-element.43.kt, f32[16,40,256]{2,1,0:T(8,128)S(1)} %all_to_all.37.got.got2), custom_call_target="tpu_custom_call" | custom-call | bytes 9437184 | tf_op jit(solution)/shard_map/pallas_call | solution.py:49
  120.4 3.6 %all-to-all-start.5 = ((f32[8,16,256]{2,1,0:T(8,128)}), f32[8,16,256]{2,1,0:T(8,128)S(1)}, u32[]{:S(2)}, u32[]{:S(2)}) async-start(f32[8,16,256]{2,1,0:T(8,128)} %get-tuple-element.47.after), calls=%async_computation.5 | async-start | bytes 262144 | tf_op jit(solution)/shard_map/all_to_all | solution.py:576
  124.0 8.4 %shard_map.94 = (f32[512,256]{1,0:T(8,128)S(1)}, f32[8,128]{1,0:T(8,128)S(1)}) custom-call(s32[4]{0:T(128)S(1)} %pad_add_fusion.s, bf16[16384,256]{1,0:T(8,128)(2,1)} %w.5, bf16[8,640,256]{2,1,0:T(8,128)(2,1)} %bitcast.19, bf16[8,640,256]{2,1,0:T(8,128)(2,1)} %collective-permute-done.5.h_other, f32[8,16,256]{2,1,0:T(8,128)S(1)} %all_to_all.36.rz, ...), custom_call_target="tpu_custom_call" | custom-call | flops 8589934592 | bytes 8388608 | tf_op jit(solution)/shard_map/pallas_call | solution.py:49
  132.4 5.2 %shard_map.95 = (f32[72,256]{1,0:T(8,128)S(1)}, f32[72,256]{1,0:T(8,128)S(1)}) custom-call(s32[4]{0:T(128)S(1)} %pad_add_fusion.s, bf16[16,512,256]{2,1,0:T(8,128)(2,1)} %get-tuple-element.42.w, bf16[1024,256]{1,0:T(8,128)(2,1)S(1)} %bitcast.15, bf16[1024,256]{1,0:T(8,128)(2,1)S(1)} %collective-permute-done.3.zb, s32[1,1]{1,0:T(1,128)} %bitcast.12.epoch, ...), custom_call_target="tpu_custom_call" | custom-call | flops 1073741824 | bytes 6291456 | tf_op jit(solution)/shard_map/pallas_call | solution.py:49
  137.6 1.5 collective-permute-start.6
  139.0 0.9 collective-permute-done.6.tin
  139.9 0.6 shard_map.96
  140.5 16.0 %all_to_all.38.got3 = f32[8,104,256]{2,1,0:T(8,128)S(1)} all-to-all(f32[8,104,256]{2,1,0:T(8,128)S(1)} %shard_map.96), channel_id=1, replica_groups=mesh['yh'=2,'z'=8,'c'=2,'yl'=2,'x'=4] {'yl','x'}, dimensions={0} | all-to-all | bytes 1703936 | tf_op jit(solution)/shard_map/all_to_all | solution.py:598
  156.5 6.7 %shard_map.97 = (f32[1,256]{1,0:T(1,128)}, f32[256,256]{1,0:T(8,128)}, f32[512,256]{1,0:T(8,128)}) custom-call(s32[4]{0:T(128)S(1)} %pad_add_fusion.s, bf16[256,256]{1,0:T(8,128)(2,1)} %sf.3, s32[2,256]{1,0:T(2,128)} %bitcast.22, s32[2,256]{1,0:T(2,128)} %bitcast.25, f32[16,16,256]{2,1,0:T(8,128)S(1)} %all_to_all.35.got.got1, ...), custom_call_target="tpu_custom_call" | custom-call | flops 1073741824 | bytes 8388608 | tf_op jit(solution)/shard_map/pallas_call | solution.py:49
  (9 shorter events, 0.1 us)
Async XLA Ops:
  9.7 15.4 %collective-permute-start = (bf16[320,256]{1,0:T(8,128)(2,1)S(1)}, bf16[320,256]{1,0:T(8,128)(2,1)S(1)}, u32[]{:S(2)}, u32[]{:S(2)}) collective-permute-start(bf16[320,256]{1,0:T(8,128)(2,1)S(1)} %get-tuple-element.31.b00), channel_id=1, source_target_pairs={{0,8},{8,0},{1,9},{9,1},{2,10},{10,2},{3,11},{11,3},{4,12},{12,4},... | collective-permute-start | bytes 491528 | tf_op jit(solution)/shard_map/ppermute | solution.py:464
  12.9 26.6 %all-to-all-start = ((bf16[16,64,256]{2,1,0:T(8,128)(2,1)}), bf16[16,64,256]{2,1,0:T(8,128)(2,1)S(1)}, u32[]{:S(2)}, u32[]{:S(2)}) async-start(bf16[16,64,256]{2,1,0:T(8,128)(2,1)} %get-tuple-element.30), calls=%async_computation | async-start | bytes 1048576 | tf_op jit(solution)/shard_map/all_to_all | solution.py:466
  22.1 92.8 %all-gather.3.cloned.1.call-start = ((), (), s32[]{:S(2)}) async-start(), calls=%async_computation.7 | async-start | bytes 2949120 | tf_op jit(solution)/shard_map/all_gather | solution.py:513
  22.2 9.8 %collective-permute-start.1 = (bf16[320,256]{1,0:T(8,128)(2,1)S(1)}, bf16[320,256]{1,0:T(8,128)(2,1)S(1)}, u32[]{:S(2)}, u32[]{:S(2)}) collective-permute-start(bf16[320,256]{1,0:T(8,128)(2,1)S(1)} %get-tuple-element.31.b00), channel_id=1, source_target_pairs={{0,128},{128,0},{1,129},{129,1},{2,130},{130,2},{3,131},{131,3},{4... | collective-permute-start | bytes 491528 | tf_op jit(solution)/shard_map/ppermute | solution.py:465
  31.9 2.2 %collective-permute-start.2 = (bf16[320,256]{1,0:T(8,128)(2,1)S(1)}, bf16[320,256]{1,0:T(8,128)(2,1)S(1)}, u32[]{:S(2)}, u32[]{:S(2)}) collective-permute-start(bf16[320,256]{1,0:T(8,128)(2,1)S(1)} %collective-permute-done.1.b10), channel_id=1, source_target_pairs={{0,8},{8,0},{1,9},{9,1},{2,10},{10,2},{3,11},{11,3},{4,12},{12,4},... | collective-permute-start | bytes 491528 | tf_op jit(solution)/shard_map/ppermute | solution.py:482
  39.6 2.0 %collective-permute-start.3 = (bf16[1024,256]{1,0:T(8,128)(2,1)S(1)}, bf16[1024,256]{1,0:T(8,128)(2,1)S(1)}, u32[]{:S(2)}, u32[]{:S(2)}) collective-permute-start(bf16[1024,256]{1,0:T(8,128)(2,1)S(1)} %bitcast.13), channel_id=1, source_target_pairs={{0,8},{8,0},{1,9},{9,1},{2,10},{10,2},{3,11},{11,3},{4,12},{12,4},... | collective-permute-start | bytes 1572872 | tf_op jit(solution)/shard_map/ppermute | solution.py:493
  48.2 15.3 %collective-permute-start.4 = (f32[528,256]{1,0:T(8,128)S(1)}, f32[528,256]{1,0:T(8,128)S(1)}, u32[]{:S(2)}, u32[]{:S(2)}) collective-permute-start(f32[528,256]{1,0:T(8,128)S(1)} %get-tuple-element.40), channel_id=1, source_target_pairs={{0,128},{128,0},{1,129},{129,1},{2,130},{130,2},{3,131},{131,3},{4... | collective-permute-start | bytes 1622024 | tf_op jit(solution)/shard_map/ppermute | solution.py:491
  51.2 14.7 %all-to-all-start.1 = ((f32[8,8,256]{2,1,0:T(8,128)}), f32[8,8,256]{2,1,0:T(8,128)S(1)}, u32[]{:S(2)}, u32[]{:S(2)}) async-start(f32[8,8,256]{2,1,0:T(8,128)} %get-tuple-element.39.after), calls=%async_computation.1 | async-start | bytes 131072 | tf_op jit(solution)/shard_map/all_to_all | solution.py:524
  115.0 9.0 %collective-permute-start.5 = (bf16[8,640,256]{2,1,0:T(8,128)(2,1)}, bf16[8,640,256]{2,1,0:T(8,128)(2,1)}, u32[]{:S(2)}, u32[]{:S(2)}) collective-permute-start(bf16[8,640,256]{2,1,0:T(8,128)(2,1)} %bitcast.18), channel_id=1, source_target_pairs={{0,8},{8,0},{1,9},{9,1},{2,10},{10,2},{3,11},{11,3},{4,12},{12,4},... | collective-permute-start | bytes 7864328 | tf_op jit(solution)/shard_map/ppermute | solution.py:553
  120.4 11.9 %all-to-all-start.5 = ((f32[8,16,256]{2,1,0:T(8,128)}), f32[8,16,256]{2,1,0:T(8,128)S(1)}, u32[]{:S(2)}, u32[]{:S(2)}) async-start(f32[8,16,256]{2,1,0:T(8,128)} %get-tuple-element.47.after), calls=%async_computation.5 | async-start | bytes 262144 | tf_op jit(solution)/shard_map/all_to_all | solution.py:576
  137.6 2.4 %collective-permute-start.6 = (f32[72,256]{1,0:T(8,128)S(1)}, f32[72,256]{1,0:T(8,128)S(1)}, u32[]{:S(2)}, u32[]{:S(2)}) collective-permute-start(f32[72,256]{1,0:T(8,128)S(1)} %get-tuple-element.51), channel_id=1, source_target_pairs={{0,8},{8,0},{1,9},{9,1},{2,10},{10,2},{3,11},{11,3},{4,12},{12,4},... | collective-permute-start | bytes 221192 | tf_op jit(solution)/shard_map/ppermute | solution.py:590
Sparse Core Ops, SparseCore 0:
  48.4 41.5 all-gather.2
where the time goes:
time: 171 us; the launch traced here: 170 us
  blocking collectives  59.4 us (35%)
  Pallas kernels  58 us (34%)
  starting transfers between devices  32.6 us (19%)
  between operations  14.8 us (9%)
  waiting for transfers between devices  5.2 us (3%)
    pallas_call x13, Pallas kernels, call(): pl.pallas_call(body, grid_spec=pltpu.PrefetchScalarGridSpec(num_scalar_pr...  58 us
    all_to_all x1, blocking collectives, local(): got2 = lax.all_to_all(pay2, prc, 0, 0, tiled=True)  16.3 us
    all_to_all x1, blocking collectives, local(): got3 = lax.all_to_all(pay3, ('yl', 'x'), 0, 0, tiled=True)  16 us
    all_to_all x1, blocking collectives, local(): got1 = lax.all_to_all(pay1, prc, 0, 0, tiled=True)  14.1 us
    all_to_all x1, blocking collectives, local(): rz2 = lax.all_to_all(rz2, 'z', 0, 0, tiled=True)  13 us
    all_to_all x1, starting transfers between devices, local(): za = lax.all_to_all(trep, ('yh', 'z'), 0, 0, tiled=True).reshape(NT // 2, D)  9.18 us
    all_to_all x1, starting transfers between devices, local(): rz1 = lax.all_to_all(rz1, 'z', 0, 0, tiled=True)  7.33 us
    all_to_all x1, starting transfers between devices, local(): rz3 = lax.all_to_all(rz3, 'z', 0, 0, tiled=True)  3.56 us
  transfers between devices with their start and end apart: 11, of which 4 were waited for; matrix products, arithmetic and copies ran while one was open for 0% of the time, Pallas kernels for 21%

commit v1 on v0

--- a/solution.py
+++ b/solution.py
@@ -169,9 +169,16 @@
         trow[pl.ds(s[0] * 2 + s[2] + 8, 1), :] = (m[0:1, :] + m[1:2, :]) * (1.0 / NP)
 
 
-def e2_body(s, w, b10, b11, trow1, send, trow, tacc, wv, si):
+def e2_body(s, w, b10, b11, trow1, b00, send, trow, group, tacc, wv, si, so):
     ins = copier(lambda j: w.at[j], lambda j: wv.at[j], si)
     start_all(Z, ins)
+    size = CR + TE
+    outs = [
+        pltpu.make_async_copy(blk, group.at[pl.ds(q * size, size), :], so.at[q])
+        for q, blk in enumerate((b00, b10))
+    ]
+    for copy in outs:
+        copy.start()
     send[...] = jnp.zeros_like(send)
     tacc[...] = jnp.zeros_like(tacc)
     for j in range(Z):
@@ -180,6 +187,8 @@
     trow[...] = trow1[...]
     put_totals(s, 1, tacc, trow)
     send[2 * CR : 2 * CR + 16, :] = trow[...]
+    for copy in outs:
+        copy.wait()
 
 
 def put_rows(racc, rsc):
@@ -187,19 +196,11 @@
         rsc[k : k + 1, :] = racc[0:1, k * 256 : (k + 1) * 256]
 
 
-def k_body(s, w, za, zb, epoch, after, b00, b10, kt, rz, group, racc, rsc, so):
+def k_body(s, w, za, zb, epoch, after, kt, rz, racc, rsc):
     i = pl.program_id(0)
-
-    size = CR + TE
-    outs = [
-        pltpu.make_async_copy(blk, group.at[pl.ds(q * size, size), :], so.at[q])
-        for q, blk in enumerate((b00, b10))
-    ]
 
     @pl.when(i == 0)
     def _():
-        for copy in outs:
-            copy.start()
         racc[...] = jnp.zeros_like(racc)
 
     tau = 0.04 + 0.001 * epoch[0:1, 0:1].astype(F32)
@@ -209,8 +210,8 @@
     half = NT // 2
     ka = jnp.exp2(dot(wb, za[...], 1, 1) * factor)
     kb = jnp.exp2(dot(wb, zb[...], 1, 1) * factor)
-    kt[0, :, 0:half] = ka
-    kt[0, :, half:NT] = kb
+    kt[0, :, 0:half] = ka.astype(BF16)
+    kt[0, :, half:NT] = kb.astype(BF16)
     c = 1.0 / (jnp.sum(ka, axis=1, keepdims=True) + jnp.sum(kb, axis=1, keepdims=True))
     racc[0:1, 0:half] += jnp.sum(ka * c, axis=0, keepdims=True)
     racc[0:1, half:NT] += jnp.sum(kb * c, axis=0, keepdims=True)
@@ -220,8 +221,6 @@
         put_rows(racc, rsc)
         for b in range(Z):
             rz[b] = rsc[...]
-        for copy in outs:
-            copy.wait()
 
 
 def mid1_body(s, rz, tpk, tin, after, out):
@@ -272,7 +271,7 @@
 
     def step(j):
         ins(j).wait()
-        k = kv[j]
+        k = kv[j].astype(F32)
         c = 1.0 / jnp.sum(k * u[...], axis=1, keepdims=True)
         racc[...] += jnp.sum(k * c, axis=0, keepdims=True)
 
@@ -292,7 +291,7 @@
 
     def step(j):
         ins(j).wait()
-        k = kv[j]
+        k = kv[j].astype(F32)
         ku = k * u[...]
         t = ku[:, 0:128]
         for a in range(1, NT // 128):
@@ -432,7 +431,7 @@
 
     def step(k):
         ks(k).wait()
-        acc = dot((kv[k] * u_all[...]).astype(BF16), hv[...])
+        acc = dot((kv[k].astype(F32) * u_all[...]).astype(BF16), hv[...])
         rows = pl.ds(k * KR, KR)
         wn, inv_w = unit(w[rows, :])
         gw = SCALE * (gwp[rows, :] - acc * cv[k, :, 0:1])
@@ -480,37 +479,36 @@
     )
     b10, trow1 = lax.optimization_barrier((b10, trow1))
     b11 = lax.ppermute(b10, "c", swap)
-    send, tpk = call(
+    send, tpk, group = call(
         e2_body, idx, 1,
-        (hbm(wnb), b10, b11, trow1),
-        [ANY] + [whole((CR + TE, D))] * 2 + [whole((16, D))],
-        [sds((2 * CR + 16, D), F32), sds((16, D), F32)],
-        [whole((2 * CR + 16, D)), whole((16, D))],
-        [tbuf, wbuf, sems(Z)], flops=4 << 30, nbytes=4 << 20,
+        (hbm(wnb), b10, b11, trow1, b00),
+        [ANY] + [whole((CR + TE, D))] * 2 + [whole((16, D)), ANY],
+        [sds((2 * CR + 16, D), F32), sds((16, D), F32), pltpu.HBM((2 * (CR + TE), D), BF16)],
+        [whole((2 * CR + 16, D)), whole((16, D)), ANY],
+        [tbuf, wbuf, sems(Z), sems(2)], flops=4 << 30, nbytes=4 << 20,
     )
     tin = lax.ppermute(send, "yh", swap)
-    za, tpk = lax.optimization_barrier((za, tpk))
+    za, tpk, group = lax.optimization_barrier((za, tpk, group))
+    h_own = lax.all_gather(group, "z", axis=0, tiled=False)
     zb = lax.ppermute(za, "c", swap)
 
-    kbuf = pltpu.VMEM((KC, KR, NT), F32)
+    kbuf = pltpu.VMEM((KC, KR, NT), BF16)
     kt_spec = spec((1, KR, NT), lambda i, s: (i, 0, 0))
     per = SH // KR
-    kt, rz1, group = call(
+    kt, rz1 = call(
         k_body, idx, KC,
-        (protos, za, zb, ep, tpk, b00, b10),
+        (protos, za, zb, ep, tpk),
         [
             spec((KR, D), lambda i, s: ((((i // per) * Z + s[1]) * C + s[2]) * per + i % per, 0)),
-            whole((NT // 2, D)), whole((NT // 2, D)), whole((1, 1)), ANY, ANY, ANY,
+            whole((NT // 2, D)), whole((NT // 2, D)), whole((1, 1)), ANY,
         ],
         [
-            pltpu.HBM((KC, KR, NT), F32), sds((Z, 8, D), F32),
-            pltpu.HBM((2 * (CR + TE), D), BF16),
+            pltpu.HBM((KC, KR, NT), BF16), sds((Z, 8, D), F32),
         ],
-        [kt_spec, whole((Z, 8, D)), ANY],
-        [pltpu.VMEM((1, NT), F32), pltpu.VMEM((8, D), F32), sems(2)],
+        [kt_spec, whole((Z, 8, D))],
+        [pltpu.VMEM((1, NT), F32), pltpu.VMEM((8, D), F32)],
         flops=4 << 30, nbytes=10 << 20,
     )
-    h_own = lax.all_gather(group, "z", axis=0, tiled=False)
     wall = pltpu.VMEM((YH * Z, SH, D), BF16)
     wnc, done = call(
         norm_body, idx, 1,
@@ -611,7 +609,7 @@
         [whole((1, CR)), whole((CR, D)), whole((SH, D))],
         [
             pltpu.VMEM((8, D), F32), pltpu.VMEM((8, D), F32), pltpu.VMEM((CR, D), F32),
-            pltpu.VMEM((NT, D), BF16), pltpu.VMEM((n, KR, NT), F32),
+            pltpu.VMEM((NT, D), BF16), pltpu.VMEM((n, KR, NT), BF16),
             pltpu.VMEM((n, KR, 128), F32), pltpu.VMEM((1, NT), F32), sems(n + 33),
         ],
         flops=1 << 30, nbytes=8 << 20,

time: 171 us -> 165 us (0.965)
  Pallas kernels: 58 us -> 54.7 us
  blocking collectives: 59.4 us -> 56.8 us
    pallas_call x13, Pallas kernels: 58 us -> 54.7 us  [call(): pl.pallas_call(body, grid_spec=pltpu.PrefetchScalarGridSpec(num_scalar_pr...]
    all_to_all x1, blocking collectives: 13 us -> 10.8 us  [local(): rz2 = lax.all_to_all(rz2, 'z', 0, 0, tiled=True)]
  transfers between devices with their start and end apart: 11 -> 11, of which waited for: 4 -> 3; matrix products, arithmetic and copies ran while one was open for 0% -> 0% of each run, Pallas kernels for 21% -> 25%
where the time goes in v1:
time: 165 us; the launch traced here: 164 us
  blocking collectives  56.8 us (34%)
  Pallas kernels  54.7 us (33%)
  starting transfers between devices  32.6 us (20%)
  between operations  14.8 us (9%)
  waiting for transfers between devices  5.08 us (3%)
    pallas_call x13, Pallas kernels, call(): pl.pallas_call(body, grid_spec=pltpu.PrefetchScalarGridSpec(num_scalar_pr...  54.7 us
    all_to_all x1, blocking collectives, local(): got2 = lax.all_to_all(pay2, prc, 0, 0, tiled=True)  16.2 us
    all_to_all x1, blocking collectives, local(): got3 = lax.all_to_all(pay3, ('yl', 'x'), 0, 0, tiled=True)  16 us
    all_to_all x1, blocking collectives, local(): got1 = lax.all_to_all(pay1, prc, 0, 0, tiled=True)  13.8 us
    all_to_all x1, blocking collectives, local(): rz2 = lax.all_to_all(rz2, 'z', 0, 0, tiled=True)  10.8 us
    all_to_all x1, starting transfers between devices, local(): za = lax.all_to_all(trep, ('yh', 'z'), 0, 0, tiled=True).reshape(NT // 2, D)  9.18 us
    all_to_all x1, starting transfers between devices, local(): rz1 = lax.all_to_all(rz1, 'z', 0, 0, tiled=True)  7.33 us
    all_to_all x1, starting transfers between devices, local(): rz3 = lax.all_to_all(rz3, 'z', 0, 0, tiled=True)  3.56 us
  transfers between devices with their start and end apart: 11, of which 3 were waited for; matrix products, arithmetic and copies ran while one was open for 0% of the time, Pallas kernels for 25%

profile of v1, /device:TPU:1, one launch (start us, length us, event | category | flops | bytes accessed | tf_op | source)
XLA Modules:
  0.0 164.1 jit_solution(17371807288203057074)
XLA Ops:
  7.2 0.1 pad_add_fusion.s
  7.3 2.5 %shard_map.85 = (bf16[320,256]{1,0:T(8,128)(2,1)S(1)}, bf16[16,64,256]{2,1,0:T(8,128)(2,1)}) custom-call(s32[4]{0:T(128)S(1)} %pad_add_fusion.s, bf16[256,256]{1,0:T(8,128)(2,1)} %sf.3, bf16[64,256]{1,0:T(8,128)(2,1)} %tf.1, s32[2,256]{1,0:T(2,128)} %bitcast.21, s32[2,256]{1,0:T(2,128)} %bitcast.23), custom_call_target="tpu_custom_call" | custom-call | bytes 1048576 | tf_op jit(solution)/shard_map/pallas_call | solution.py:49
  9.7 3.2 %collective-permute-start = (bf16[320,256]{1,0:T(8,128)(2,1)S(1)}, bf16[320,256]{1,0:T(8,128)(2,1)S(1)}, u32[]{:S(2)}, u32[]{:S(2)}) collective-permute-start(bf16[320,256]{1,0:T(8,128)(2,1)S(1)} %get-tuple-element.32.b00), channel_id=1, source_target_pairs={{0,8},{8,0},{1,9},{9,1},{2,10},{10,2},{3,11},{11,3},{4,12},{12,4},... | collective-permute-start | bytes 491528 | tf_op jit(solution)/shard_map/ppermute | solution.py:463
  12.9 9.2 %all-to-all-start = ((bf16[16,64,256]{2,1,0:T(8,128)(2,1)}), bf16[16,64,256]{2,1,0:T(8,128)(2,1)S(1)}, u32[]{:S(2)}, u32[]{:S(2)}) async-start(bf16[16,64,256]{2,1,0:T(8,128)(2,1)} %get-tuple-element.31), calls=%async_computation | async-start | bytes 1048576 | tf_op jit(solution)/shard_map/all_to_all | solution.py:465
  22.1 0.0 all-gather.3.cloned.1.call-start
  22.2 3.0 %collective-permute-start.1 = (bf16[320,256]{1,0:T(8,128)(2,1)S(1)}, bf16[320,256]{1,0:T(8,128)(2,1)S(1)}, u32[]{:S(2)}, u32[]{:S(2)}) collective-permute-start(bf16[320,256]{1,0:T(8,128)(2,1)S(1)} %get-tuple-element.32.b00), channel_id=1, source_target_pairs={{0,128},{128,0},{1,129},{129,1},{2,130},{130,2},{3,131},{131,3},{4... | collective-permute-start | bytes 491528 | tf_op jit(solution)/shard_map/ppermute | solution.py:464
  25.1 6.8 %shard_map.86 = (f32[512,256]{1,0:T(8,128)S(1)}, f32[16,256]{1,0:T(8,128)S(1)}, bf16[8,512,256]{2,1,0:T(8,128)(2,1)}) custom-call(s32[4]{0:T(128)S(1)} %pad_add_fusion.s, bf16[16,2,512,256]{3,2,1,0:T(8,128)(2,1)} %bitcast.16, bf16[320,256]{1,0:T(8,128)(2,1)S(1)} %get-tuple-element.32.b00, bf16[320,256]{1,0:T(8,128)(2,1)S(1)} %collective-permute-done.b01, ...), custom_call_target="tpu_custom_call" | custom-call | flops 4294967296 | bytes 4194304 | tf_op jit(solution)/shard_map/pallas_call | solution.py:49
  31.9 1.2 collective-permute-start.2
  33.1 1.0 collective-permute-done.2.b11
  34.1 5.4 %shard_map.87 = (f32[528,256]{1,0:T(8,128)S(1)}, f32[16,256]{1,0:T(8,128)S(1)}, bf16[640,256]{1,0:T(8,128)(2,1)}) custom-call(s32[4]{0:T(128)S(1)} %pad_add_fusion.s, bf16[8,512,256]{2,1,0:T(8,128)(2,1)} %get-tuple-element.33.w, bf16[320,256]{1,0:T(8,128)(2,1)S(1)} %collective-permute-done.1.b10, bf16[320,256]{1,0:T(8,128)(2,1)S(1)} %collective-permute-done.2.b11, ...), custom_call_target="tpu_custom_call" | custom-call | flops 4294967296 | bytes 4194304 | tf_op jit(solution)/shard_map/pallas_call | solution.py:49
  39.6 0.5 collective-permute-start.3
  40.8 2.9 %collective-permute-start.4 = (f32[528,256]{1,0:T(8,128)S(1)}, f32[528,256]{1,0:T(8,128)S(1)}, u32[]{:S(2)}, u32[]{:S(2)}) collective-permute-start(f32[528,256]{1,0:T(8,128)S(1)} %get-tuple-element.42), channel_id=1, source_target_pairs={{0,128},{128,0},{1,129},{129,1},{2,130},{130,2},{3,131},{131,3},{4... | collective-permute-start | bytes 1622024 | tf_op jit(solution)/shard_map/ppermute | solution.py:490
  43.7 5.9 %shard_map.88 = (bf16[4,256,2048]{2,1,0:T(8,128)(2,1)}, f32[8,8,256]{2,1,0:T(8,128)}) custom-call(s32[4]{0:T(128)S(1)} %pad_add_fusion.s, bf16[16384,256]{1,0:T(8,128)(2,1)} %w.5, bf16[1024,256]{1,0:T(8,128)(2,1)S(1)} %bitcast.14, bf16[1024,256]{1,0:T(8,128)(2,1)S(1)} %collective-permute-done.3.zb, s32[1,1]{1,0:T(1,128)} %bitcast.11.epoch, ...), custom_call_target="tpu_custom_call" | custom-call | flops 4294967296 | bytes 10485760 | tf_op jit(solution)/shard_map/pallas_call | solution.py:49
  49.6 7.3 %all-to-all-start.1 = ((f32[8,8,256]{2,1,0:T(8,128)}), f32[8,8,256]{2,1,0:T(8,128)S(1)}, u32[]{:S(2)}, u32[]{:S(2)}) async-start(f32[8,8,256]{2,1,0:T(8,128)} %get-tuple-element.41.after), calls=%async_computation.1 | async-start | bytes 131072 | tf_op jit(solution)/shard_map/all_to_all | solution.py:522
  56.9 5.0 %shard_map.89 = (bf16[16,512,256]{2,1,0:T(8,128)(2,1)}, f32[8,128]{1,0:T(8,128)S(1)}) custom-call(s32[4]{0:T(128)S(1)} %pad_add_fusion.s, bf16[16,2,512,256]{3,2,1,0:T(8,128)(2,1)} %bitcast.17, f32[8,8,256]{2,1,0:T(8,128)} %get-tuple-element.41.after), custom_call_target="tpu_custom_call" | custom-call | flops 2147483648 | bytes 8388608 | tf_op jit(solution)/shard_map/pallas_call | solution.py:49
  61.9 3.1 %all-to-all-done.1.rz = f32[8,8,256]{2,1,0:T(8,128)S(1)} async-done(((f32[8,8,256]{2,1,0:T(8,128)}), f32[8,8,256]{2,1,0:T(8,128)S(1)}, u32[]{:S(2)}, u32[]{:S(2)}) %all-to-all-start.1) | async-done | bytes 65568 | tf_op jit(solution)/shard_map/all_to_all | solution.py:522
  65.0 0.6 shard_map.90
  65.6 13.8 %all_to_all.35.got.got1 = f32[16,16,256]{2,1,0:T(8,128)S(1)} all-to-all(f32[16,16,256]{2,1,0:T(8,128)S(1)} %shard_map.90), channel_id=1, replica_groups=mesh['yh'=2,'z'=8,'c'=2,'yl'=2,'x'=4] {'c','yl','x'}, dimensions={0} | all-to-all | bytes 524288 | tf_op jit(solution)/shard_map/all_to_all | solution.py:530
  79.4 3.4 %shard_map.91 = f32[8,16,256]{2,1,0:T(8,128)S(1)} custom-call(s32[4]{0:T(128)S(1)} %pad_add_fusion.s, bf16[4,256,2048]{2,1,0:T(8,128)(2,1)} %get-tuple-element.45.kt, f32[16,16,256]{2,1,0:T(8,128)S(1)} %all_to_all.35.got.got1), custom_call_target="tpu_custom_call" | custom-call | bytes 9437184 | tf_op jit(solution)/shard_map/pallas_call | solution.py:49
  82.8 10.8 %all_to_all.36.rz = f32[8,16,256]{2,1,0:T(8,128)S(1)} all-to-all(f32[8,16,256]{2,1,0:T(8,128)S(1)} %shard_map.91), channel_id=1, replica_groups=mesh['yh'=2,'z'=8,'c'=2,'yl'=2,'x'=4] {'z'}, dimensions={0} | all-to-all | bytes 262144 | tf_op jit(solution)/shard_map/all_to_all | solution.py:540
  93.6 0.6 shard_map.92
  94.2 16.2 %all_to_all.37.got.got2 = f32[16,40,256]{2,1,0:T(8,128)S(1)} all-to-all(f32[16,40,256]{2,1,0:T(8,128)S(1)} %shard_map.92), channel_id=1, replica_groups=mesh['yh'=2,'z'=8,'c'=2,'yl'=2,'x'=4] {'c','yl','x'}, dimensions={0} | all-to-all | bytes 1310720 | tf_op jit(solution)/shard_map/all_to_all | solution.py:549
  110.5 0.3 collective-permute-start.5
  110.7 4.3 %shard_map.93 = (f32[8,16,256]{2,1,0:T(8,128)}, f32[4,256,128]{2,1,0:T(8,128)}) custom-call(s32[4]{0:T(128)S(1)} %pad_add_fusion.s, bf16[4,256,2048]{2,1,0:T(8,128)(2,1)} %get-tuple-element.45.kt, f32[16,40,256]{2,1,0:T(8,128)S(1)} %all_to_all.37.got.got2), custom_call_target="tpu_custom_call" | custom-call | bytes 9437184 | tf_op jit(solution)/shard_map/pallas_call | solution.py:49
  115.1 3.6 %all-to-all-start.5 = ((f32[8,16,256]{2,1,0:T(8,128)}), f32[8,16,256]{2,1,0:T(8,128)S(1)}, u32[]{:S(2)}, u32[]{:S(2)}) async-start(f32[8,16,256]{2,1,0:T(8,128)} %get-tuple-element.49.after), calls=%async_computation.5 | async-start | bytes 262144 | tf_op jit(solution)/shard_map/all_to_all | solution.py:574
  118.7 8.4 %shard_map.94 = (f32[512,256]{1,0:T(8,128)S(1)}, f32[8,128]{1,0:T(8,128)S(1)}) custom-call(s32[4]{0:T(128)S(1)} %pad_add_fusion.s, bf16[16384,256]{1,0:T(8,128)(2,1)} %w.5, bf16[8,640,256]{2,1,0:T(8,128)(2,1)} %bitcast.19, bf16[8,640,256]{2,1,0:T(8,128)(2,1)} %collective-permute-done.5.h_other, f32[8,16,256]{2,1,0:T(8,128)S(1)} %all_to_all.36.rz, ...), custom_call_target="tpu_custom_call" | custom-call | flops 8589934592 | bytes 8388608 | tf_op jit(solution)/shard_map/pallas_call | solution.py:49
  127.1 5.2 %shard_map.95 = (f32[72,256]{1,0:T(8,128)S(1)}, f32[72,256]{1,0:T(8,128)S(1)}) custom-call(s32[4]{0:T(128)S(1)} %pad_add_fusion.s, bf16[16,512,256]{2,1,0:T(8,128)(2,1)} %get-tuple-element.44.w, bf16[1024,256]{1,0:T(8,128)(2,1)S(1)} %bitcast.15, bf16[1024,256]{1,0:T(8,128)(2,1)S(1)} %collective-permute-done.3.zb, s32[1,1]{1,0:T(1,128)} %bitcast.12.epoch, ...), custom_call_target="tpu_custom_call" | custom-call | flops 1073741824 | bytes 6291456 | tf_op jit(solution)/shard_map/pallas_call | solution.py:49
  132.2 1.4 collective-permute-start.6
  133.7 0.9 collective-permute-done.6.tin
  134.6 0.6 shard_map.96
  135.2 16.0 %all_to_all.38.got3 = f32[8,104,256]{2,1,0:T(8,128)S(1)} all-to-all(f32[8,104,256]{2,1,0:T(8,128)S(1)} %shard_map.96), channel_id=1, replica_groups=mesh['yh'=2,'z'=8,'c'=2,'yl'=2,'x'=4] {'yl','x'}, dimensions={0} | all-to-all | bytes 1703936 | tf_op jit(solution)/shard_map/all_to_all | solution.py:596
  151.2 6.1 %shard_map.97 = (f32[1,256]{1,0:T(1,128)}, f32[256,256]{1,0:T(8,128)}, f32[512,256]{1,0:T(8,128)}) custom-call(s32[4]{0:T(128)S(1)} %pad_add_fusion.s, bf16[256,256]{1,0:T(8,128)(2,1)} %sf.3, s32[2,256]{1,0:T(2,128)} %bitcast.22, s32[2,256]{1,0:T(2,128)} %bitcast.25, f32[16,16,256]{2,1,0:T(8,128)S(1)} %all_to_all.35.got.got1, ...), custom_call_target="tpu_custom_call" | custom-call | flops 1073741824 | bytes 8388608 | tf_op jit(solution)/shard_map/pallas_call | solution.py:49
  (9 shorter events, 0.0 us)
Async XLA Ops:
  9.7 15.4 %collective-permute-start = (bf16[320,256]{1,0:T(8,128)(2,1)S(1)}, bf16[320,256]{1,0:T(8,128)(2,1)S(1)}, u32[]{:S(2)}, u32[]{:S(2)}) collective-permute-start(bf16[320,256]{1,0:T(8,128)(2,1)S(1)} %get-tuple-element.32.b00), channel_id=1, source_target_pairs={{0,8},{8,0},{1,9},{9,1},{2,10},{10,2},{3,11},{11,3},{4,12},{12,4},... | collective-permute-start | bytes 491528 | tf_op jit(solution)/shard_map/ppermute | solution.py:463
  12.9 26.6 %all-to-all-start = ((bf16[16,64,256]{2,1,0:T(8,128)(2,1)}), bf16[16,64,256]{2,1,0:T(8,128)(2,1)S(1)}, u32[]{:S(2)}, u32[]{:S(2)}) async-start(bf16[16,64,256]{2,1,0:T(8,128)(2,1)} %get-tuple-element.31), calls=%async_computation | async-start | bytes 1048576 | tf_op jit(solution)/shard_map/all_to_all | solution.py:465
  22.1 88.3 %all-gather.3.cloned.1.call-start = ((), (), s32[]{:S(2)}) async-start(), calls=%async_computation.7 | async-start | bytes 2949120 | tf_op jit(solution)/shard_map/all_gather | solution.py:492
  22.2 9.8 %collective-permute-start.1 = (bf16[320,256]{1,0:T(8,128)(2,1)S(1)}, bf16[320,256]{1,0:T(8,128)(2,1)S(1)}, u32[]{:S(2)}, u32[]{:S(2)}) collective-permute-start(bf16[320,256]{1,0:T(8,128)(2,1)S(1)} %get-tuple-element.32.b00), channel_id=1, source_target_pairs={{0,128},{128,0},{1,129},{129,1},{2,130},{130,2},{3,131},{131,3},{4... | collective-permute-start | bytes 491528 | tf_op jit(solution)/shard_map/ppermute | solution.py:464
  31.9 2.2 %collective-permute-start.2 = (bf16[320,256]{1,0:T(8,128)(2,1)S(1)}, bf16[320,256]{1,0:T(8,128)(2,1)S(1)}, u32[]{:S(2)}, u32[]{:S(2)}) collective-permute-start(bf16[320,256]{1,0:T(8,128)(2,1)S(1)} %collective-permute-done.1.b10), channel_id=1, source_target_pairs={{0,8},{8,0},{1,9},{9,1},{2,10},{10,2},{3,11},{11,3},{4,12},{12,4},... | collective-permute-start | bytes 491528 | tf_op jit(solution)/shard_map/ppermute | solution.py:481
  39.6 4.1 %collective-permute-start.3 = (bf16[1024,256]{1,0:T(8,128)(2,1)S(1)}, bf16[1024,256]{1,0:T(8,128)(2,1)S(1)}, u32[]{:S(2)}, u32[]{:S(2)}) collective-permute-start(bf16[1024,256]{1,0:T(8,128)(2,1)S(1)} %bitcast.13), channel_id=1, source_target_pairs={{0,8},{8,0},{1,9},{9,1},{2,10},{10,2},{3,11},{11,3},{4,12},{12,4},... | collective-permute-start | bytes 1572872 | tf_op jit(solution)/shard_map/ppermute | solution.py:493
  40.8 21.2 %collective-permute-start.4 = (f32[528,256]{1,0:T(8,128)S(1)}, f32[528,256]{1,0:T(8,128)S(1)}, u32[]{:S(2)}, u32[]{:S(2)}) collective-permute-start(f32[528,256]{1,0:T(8,128)S(1)} %get-tuple-element.42), channel_id=1, source_target_pairs={{0,128},{128,0},{1,129},{129,1},{2,130},{130,2},{3,131},{131,3},{4... | collective-permute-start | bytes 1622024 | tf_op jit(solution)/shard_map/ppermute | solution.py:490
  49.6 15.4 %all-to-all-start.1 = ((f32[8,8,256]{2,1,0:T(8,128)}), f32[8,8,256]{2,1,0:T(8,128)S(1)}, u32[]{:S(2)}, u32[]{:S(2)}) async-start(f32[8,8,256]{2,1,0:T(8,128)} %get-tuple-element.41.after), calls=%async_computation.1 | async-start | bytes 131072 | tf_op jit(solution)/shard_map/all_to_all | solution.py:522
  110.5 8.2 %collective-permute-start.5 = (bf16[8,640,256]{2,1,0:T(8,128)(2,1)}, bf16[8,640,256]{2,1,0:T(8,128)(2,1)}, u32[]{:S(2)}, u32[]{:S(2)}) collective-permute-start(bf16[8,640,256]{2,1,0:T(8,128)(2,1)} %bitcast.18), channel_id=1, source_target_pairs={{0,8},{8,0},{1,9},{9,1},{2,10},{10,2},{3,11},{11,3},{4,12},{12,4},... | collective-permute-start | bytes 7864328 | tf_op jit(solution)/shard_map/ppermute | solution.py:551
  115.1 12.0 %all-to-all-start.5 = ((f32[8,16,256]{2,1,0:T(8,128)}), f32[8,16,256]{2,1,0:T(8,128)S(1)}, u32[]{:S(2)}, u32[]{:S(2)}) async-start(f32[8,16,256]{2,1,0:T(8,128)} %get-tuple-element.49.after), calls=%async_computation.5 | async-start | bytes 262144 | tf_op jit(solution)/shard_map/all_to_all | solution.py:574
  132.2 2.3 %collective-permute-start.6 = (f32[72,256]{1,0:T(8,128)S(1)}, f32[72,256]{1,0:T(8,128)S(1)}, u32[]{:S(2)}, u32[]{:S(2)}) collective-permute-start(f32[72,256]{1,0:T(8,128)S(1)} %get-tuple-element.53), channel_id=1, source_target_pairs={{0,8},{8,0},{1,9},{9,1},{2,10},{10,2},{3,11},{11,3},{4,12},{12,4},... | collective-permute-start | bytes 221192 | tf_op jit(solution)/shard_map/ppermute | solution.py:588
Sparse Core Ops, SparseCore 0:
  39.7 43.2 all-gather.2
